TPU v7x, 32 devices: a whole 2x2x4 slice. The times are simulated.
32 devices in a mesh: grp: 2 (over x), row: 8 (over z, y), case: 2 (over core).
Axes of the slice: x: 2, y: 2, z: 4, core: 2. Of those that a mesh axis runs over, the one named last changes fastest.
Arguments:
- snapshots: float32 [4, 512, 4096], P(('grp', 'case'), 'row'), parts along dimension 0
- counts: int32 [4], P(('grp', 'case')), parts along dimension 0, may hold values from 256 to 512, as said below
- sketch: float32 [2, 512, 128], P('case'), may hold values from -6 to 6
- start_block: float32 [256, 128], replicated, may hold values from -6 to 6
Outputs:
- case_bases: float32 [4, 128, 4096], P(('grp', 'case'), None, 'row'), parts along dimension 0
- merged: float32 [256, 4096], P('grp', ('row', 'case')), parts along dimension 0
There are 2 independent parts, one for each index of `grp`. A program takes and returns all parts, laid end to end along the dimension named above; an argument that names none is the same for every part. Nothing has to cross between parts.
Inputs may be any that keep to these rules, and one draw needn't show every extreme that they name: `counts`: one case of each part has all 512 snapshots valid; the valid snapshots of a case come first.
All inputs are finite; a program needn't handle non-finite values.
Results may differ from a plain program's by a relative error of at most 0.0003.
Values sent between devices are 32-bit elements; how exact they have to be, the bound alone decides.
No kernel may reach another device: no remote copies, remote signals or barrier semaphores. Data moves between devices by JAX's collectives and lax.ppermute only.
A program may use at most 128 MiB of HBM per device.

v0:
```python
import math

import jax
import jax.numpy as jnp
from jax import lax
from jax.sharding import PartitionSpec as P

ITERS = 2


def swapped(value, axis, apart):
    mask = 2**apart
    pairs = [(source, source ^ mask) for source in range(lax.axis_size(axis))]
    return lax.ppermute(value, axis, pairs)


def lower_solve(factor, matrix):
    return jax.scipy.linalg.solve_triangular(factor, matrix, lower=True)


def local(snapshots, counts, sketch, start_block):
    precise = lax.Precision.HIGHEST
    row_data = lax.all_to_all(snapshots, "row", split_axis=2, concat_axis=1, tiled=True)[0]
    total_steps = row_data.shape[0]
    local_edges = row_data.shape[1]
    scale_out = math.sqrt(lax.axis_size("row") * local_edges)
    edge_count = float(lax.axis_size("row") * local_edges)
    valid_mask = (lax.iota(jnp.int32, total_steps) < counts[0]).astype(jnp.float32)
    active = row_data * valid_mask[:, None]
    sketch_rows = jnp.dot(sketch[0].T, active, precision=precise)
    gram_one = lax.psum(jnp.dot(sketch_rows, sketch_rows.T, precision=precise), "row")
    ortho_one = lower_solve(jnp.linalg.cholesky(gram_one), sketch_rows)
    projected = lax.psum(jnp.dot(active, ortho_one.T, precision=precise), "row")
    powered = jnp.dot(projected.T, active, precision=precise) / edge_count
    gram_two = lax.psum(jnp.dot(powered, powered.T, precision=precise), "row")
    case_q = lower_solve(jnp.linalg.cholesky(gram_two), powered)
    case_out = (case_q * scale_out)[None]
    partner = swapped(powered, "case", 0)
    my_index = lax.axis_index("case")
    stacked = jnp.where(
        my_index == 0,
        jnp.concatenate([powered, partner], axis=0),
        jnp.concatenate([partner, powered], axis=0),
    )
    kernel = lax.psum(jnp.dot(stacked, stacked.T, precision=precise), "row")
    vectors = start_block
    for sweep_index in range(ITERS):
        vectors = jnp.dot(kernel, vectors, precision=precise)
        chol_v = jnp.linalg.cholesky(jnp.dot(vectors.T, vectors, precision=precise))
        vectors = lower_solve(chol_v, vectors.T).T
    reduced = jnp.dot(vectors.T, jnp.dot(kernel, vectors, precision=precise), precision=precise)
    chol_m = jnp.linalg.cholesky(reduced)
    half_edges = local_edges // 2
    own_cols = lax.dynamic_slice_in_dim(stacked, my_index * half_edges, half_edges, 1)
    merged = lower_solve(chol_m, jnp.dot(vectors.T, own_cols, precision=precise)) * scale_out
    return (case_out, merged)


def solution(mesh):
    in_specs = (P(("grp", "case"), "row", None), P(("grp", "case")), P("case", None, None), P())
    out_specs = (P(("grp", "case"), None, "row"), P("grp", ("row", "case")))
    return jax.shard_map(local, mesh=mesh, in_specs=in_specs, out_specs=out_specs, check_vma=False)
```

profile of v0, /device:TPU:0, one launch (start us, length us, event | category | flops | bytes accessed | tf_op | source)
XLA Modules:
  0.0 425.7 jit_solution(4059574520041455201)
XLA Ops:
  7.2 4.9 %copy.40 = f32[1,64,4096]{1,0,2:T(1,128)S(1)} copy(f32[1,64,4096]{2,1,0:T(8,128)} %param.9) | data formatting | bytes 2097152 | tf_op args[0]
  12.6 19.4 %reduce.4 = f32[4096,64]{1,0:T(8,128)} reduce(f32[4096,1,64]{2,1,0:T(1,128)S(1)} %bitcast.98, f32[]{:T(128)} %broadcast.59), dimensions={1}, to_apply=%bitcast.66.reduce_sub_computation | reduce | bytes 2097156
  32.0 3.4 reshape.30
  35.3 7.3 %all-to-all-start = ((f32[8,1,32768]{2,1,0:T(1,128)}), f32[8,1,32768]{2,1,0:T(1,128)S(1)}, u32[]{:S(2)}, u32[]{:S(2)}) async-start(f32[8,1,32768]{2,1,0:T(1,128)} %reshape.30), calls=%async_computation | async-start | bytes 2097152 | tf_op jit(solution)/shard_map/all_to_all | solution.py:23
  43.7 24.7 %all-to-all-done = f32[8,1,32768]{2,1,0:T(1,128)S(1)} async-done(((f32[8,1,32768]{2,1,0:T(1,128)}), f32[8,1,32768]{2,1,0:T(1,128)S(1)}, u32[]{:S(2)}, u32[]{:S(2)}) %all-to-all-start) | async-done | bytes 1048608 | tf_op jit(solution)/shard_map/all_to_all | solution.py:23
  68.4 3.1 reduce.5
  71.5 2.6 reshape.31
  75.8 1.8 fusion.3
  80.2 66.3 %all-reduce.5.cloned.1.call-done = f32[128,128]{0,1:T(8,128)} async-done(((f32[128,128]{0,1:T(8,128)}), f32[128,128]{0,1:T(8,128)}) %all-reduce.5.cloned.1.call-update) | async-done | bytes 65552 | tf_op jit(solution)/shard_map/psum | solution.py:31
  148.3 11.7 %cholesky.89 = f32[128,128]{1,0:T(8,128)S(1)} custom-call(f32[128,128]{1,0:T(8,128)S(1)} %fusion.25), custom_call_target="Cholesky" | custom-call | tf_op jit(solution)/shard_map/jit(cholesky)/cholesky | solution.py:32
  161.3 9.8 %custom-call.11 = f32[1,128,128]{1,2,0:T(8,128)S(1)} custom-call(f32[1,128,128]{2,1,0:T(8,128)S(1)} %fusion.11), custom_call_target="InvertDiagBlocksLowerTriangular" | custom-call | tf_op jit(solution)/shard_map/jit(_solve_triangular)/triangular_solve | solution.py:18
  171.6 1.7 fusion.32
  173.5 70.4 %all-reduce.7.cloned.1.call-done = f32[512,128]{1,0:T(8,128)} async-done(((f32[512,128]{1,0:T(8,128)}), f32[512,128]{1,0:T(8,128)}) %all-reduce.7.cloned.1.call-update) | async-done | bytes 262160 | tf_op jit(solution)/shard_map/psum | solution.py:33
  243.9 1.7 convolution_multiply_fusion.1
  248.7 70.6 %all-reduce.9.cloned.1.call-done = (f32[128,128]{0,1:T(8,128)}, f32[256,256]{1,0:T(8,128)}) async-done(((f32[128,128]{0,1:T(8,128)}, f32[256,256]{1,0:T(8,128)}), (f32[128,128]{0,1:T(8,128)}, f32[256,256]{1,0:T(8,128)})) %all-reduce.9.cloned.1.call-update) | async-done | bytes 327696 | tf_op jit(solution)/shard_map/psum | solution.py:35
  319.3 1.4 fusion.35
  321.2 11.7 %cholesky.111 = f32[128,128]{1,0:T(8,128)S(1)} custom-call(f32[128,128]{1,0:T(8,128)S(1)} %fusion.21), custom_call_target="Cholesky" | custom-call | tf_op jit(solution)/shard_map/jit(cholesky)/cholesky | solution.py:49
  334.2 9.8 %custom-call.13 = f32[1,128,128]{1,2,0:T(8,128)S(1)} custom-call(f32[1,128,128]{2,1,0:T(8,128)S(1)} %fusion.13), custom_call_target="InvertDiagBlocksLowerTriangular" | custom-call | tf_op jit(solution)/shard_map/jit(_solve_triangular)/triangular_solve | solution.py:18
  346.2 11.9 %cholesky.122 = f32[128,128]{1,0:T(8,128)S(1)} custom-call(f32[128,128]{1,0:T(8,128)S(1)} %fusion.19), custom_call_target="Cholesky" | custom-call | tf_op jit(solution)/shard_map/jit(cholesky)/cholesky | solution.py:49
  359.5 9.8 %custom-call.14 = f32[1,128,128]{1,2,0:T(8,128)S(1)} custom-call(f32[1,128,128]{2,1,0:T(8,128)S(1)} %fusion.14), custom_call_target="InvertDiagBlocksLowerTriangular" | custom-call | tf_op jit(solution)/shard_map/jit(_solve_triangular)/triangular_solve | solution.py:18
  370.4 11.7 %cholesky.133 = f32[128,128]{1,0:T(8,128)S(1)} custom-call(f32[128,128]{1,0:T(8,128)S(1)} %fusion.17), custom_call_target="Cholesky" | custom-call | tf_op jit(solution)/shard_map/jit(cholesky)/cholesky | solution.py:52
  383.4 9.8 %custom-call.15 = f32[1,128,128]{1,2,0:T(8,128)S(1)} custom-call(f32[1,128,128]{2,1,0:T(8,128)S(1)} %fusion.15), custom_call_target="InvertDiagBlocksLowerTriangular" | custom-call | tf_op jit(solution)/shard_map/jit(_solve_triangular)/triangular_solve | solution.py:18
  393.7 11.9 %cholesky.100 = f32[128,128]{1,0:T(8,128)S(1)} custom-call(f32[128,128]{1,0:T(8,128)S(1)} %fusion.23), custom_call_target="Cholesky" | custom-call | tf_op jit(solution)/shard_map/jit(cholesky)/cholesky | solution.py:36
  407.0 9.8 %custom-call.12 = f32[1,128,128]{1,2,0:T(8,128)S(1)} custom-call(f32[1,128,128]{2,1,0:T(8,128)S(1)} %fusion.12), custom_call_target="InvertDiagBlocksLowerTriangular" | custom-call | tf_op jit(solution)/shard_map/jit(_solve_triangular)/triangular_solve | solution.py:18
  (65 shorter events, 23.4 us)
Async XLA Ops:
  7.2 68.6 %copy-start = (f32[1,512,128]{2,1,0:T(8,128)S(1)}, f32[1,512,128]{2,1,0:T(8,128)}, u32[]{:S(2)}) copy-start(f32[1,512,128]{2,1,0:T(8,128)} %param.11) | copy-start | bytes 786436
  35.3 33.0 %all-to-all-start = ((f32[8,1,32768]{2,1,0:T(1,128)}), f32[8,1,32768]{2,1,0:T(1,128)S(1)}, u32[]{:S(2)}, u32[]{:S(2)}) async-start(f32[8,1,32768]{2,1,0:T(1,128)} %reshape.30), calls=%async_computation | async-start | bytes 2097152 | tf_op jit(solution)/shard_map/all_to_all | solution.py:23
  42.6 103.9 %all-reduce.5.cloned.1.call-start = ((), (), s32[]{:S(2)}) async-start(), calls=%async_computation.1 | async-start | bytes 131072 | tf_op jit(solution)/shard_map/psum | solution.py:31
  78.8 165.1 %all-reduce.7.cloned.1.call-start = ((), (), s32[]{:S(2)}) async-start(), calls=%async_computation.2 | async-start | bytes 524288 | tf_op jit(solution)/shard_map/psum | solution.py:33
  173.3 146.0 %copy-start.3 = (f32[256,128]{1,0:T(8,128)S(1)}, f32[256,128]{1,0:T(8,128)}, u32[]{:S(2)}) copy-start(f32[256,128]{1,0:T(8,128)} %param.12) | copy-start | bytes 393220
  173.3 146.0 %all-reduce.9.cloned.1.call-start = ((), (), s32[]{:S(2)}) async-start(), calls=%async_computation.3 | async-start | bytes 655360 | tf_op jit(solution)/shard_map/psum | solution.py:35
  245.7 1.6 collective-permute-start
  319.3 50.3 %copy-start.1 = (f32[256,256]{1,0:T(8,128)S(1)}, f32[256,256]{1,0:T(8,128)}, u32[]{:S(2)}) copy-start(f32[256,256]{1,0:T(8,128)} %get-tuple-element.6) | copy-start | bytes 786436
  321.2 72.4 %copy-start.2 = (f32[128,128]{0,1:T(8,128)S(1)}, f32[128,128]{0,1:T(8,128)}, u32[]{:S(2)}) copy-start(f32[128,128]{0,1:T(8,128)} %get-tuple-element.4) | copy-start | bytes 196612
Sparse Core Ops, SparseCore 0:
  79.0 67.4 all-reduce.4
  173.4 70.5 all-reduce.6
  248.8 70.4 all-reduce.8
where the time goes:
time: 430 us; the launch traced here: 426 us
  waiting for transfers between devices  233 us (54%)
  other arithmetic  138 us (32%)
  matrix products  16.3 us (4%)
  between operations  15 us (3%)
  local copies, waits for them, and re-layouts  14.9 us (3%)
  starting transfers between devices  8.46 us (2%)
    psum x1, waiting for transfers between devices, local(): gram_two = lax.psum(jnp.dot(powered, powered.T, precision=precise), 'row')  70.6 us
    psum x1, waiting for transfers between devices, local(): projected = lax.psum(jnp.dot(active, ortho_one.T, precision=precise), 'row')  70.4 us
    psum x1, waiting for transfers between devices, local(): lax.psum(jnp.dot(sketch_rows, sketch_rows.T, precision=precise), 'row')  66.3 us
    another operation x10, other arithmetic, lower_solve(): return jax.scipy.linalg.solve_triangular(factor, matrix, lower=True)  52.3 us
    another operation x6, other arithmetic, local(): chol_v = jnp.linalg.cholesky(jnp.dot(vectors.T, vectors, precision=precise))  25 us
    all_to_all x1, waiting for transfers between devices, local(): lax.all_to_all(snapshots, 'row', split_axis=2, concat_axis=1, tiled=True)[0]  24.7 us
    unnamed x1, other arithmetic  19.4 us
    another operation x3, other arithmetic, local(): case_q = lower_solve(jnp.linalg.cholesky(gram_two), powered)  12.6 us
  transfers between devices with their start and end apart: 5, of which 5 were waited for; matrix products, arithmetic and copies ran while one was open for 0% of the time, Pallas kernels for 0%

commit v1 on v0

v1 whole, which is shorter than its diff:
```python
import functools
import math

import jax
import jax.numpy as jnp
from jax import lax
from jax.experimental import pallas as pl
from jax.experimental.pallas import tpu as pltpu
from jax.sharding import PartitionSpec as P

ITERS = 2
TILE = 8
VMEM_BYTES = 32 * 1024 * 1024
precise = lax.Precision.HIGHEST


def dot(a, b, contract=(1, 0)):
    dims = (((contract[0],), (contract[1],)), ((), ()))
    return lax.dot_general(a, b, dims, precision=precise, preferred_element_type=jnp.float32)


def row_copies(value, row):
    return jnp.broadcast_to(value[row : row + 1, :], value.shape)


def inverse_cholesky(mats):
    size = mats[0].shape[0]
    tiles = size // TILE
    lane = lax.broadcasted_iota(jnp.int32, (TILE, size), 1)
    sublane = lax.broadcasted_iota(jnp.int32, (TILE, size), 0)
    stacks = [[m[TILE * i : TILE * (i + 1), :] for i in range(tiles)] for m in mats]
    for t in range(tiles):
        first = TILE * t
        in_panel = (lane >= first) & (lane < first + TILE)
        eye = (lane - first == sublane).astype(jnp.float32)
        for rows in stacks:
            column = lambda i, c: jnp.broadcast_to(rows[i][:, first + c : first + c + 1], (TILE, size))
            diag = [column(t, c) for c in range(TILE)]
            full = jnp.where(in_panel, eye, rows[t])
            factor = full
            for j in range(TILE):
                pivot = row_copies(diag[j], j)
                inverse = 1.0 / pivot
                here = sublane == j
                line = row_copies(full, j)
                factor = jnp.where(here, line * lax.rsqrt(pivot), factor)
                line = line * inverse
                full = jnp.where(here, line, full - diag[j] * line)
                for c in range(j + 1, TILE):
                    entry = row_copies(diag[c], j) * inverse
                    diag[c] = jnp.where(here, entry, diag[c] - diag[j] * entry)
            lines = [row_copies(full, c) for c in range(TILE)]
            for i in range(t + 1, tiles):
                total = jnp.where(in_panel, 0.0, rows[i])
                for c in range(TILE):
                    total = total - column(i, c) * lines[c]
                rows[i] = total
            rows[t] = factor
    lower = lax.broadcasted_iota(jnp.int32, (size, size), 1) <= lax.broadcasted_iota(jnp.int32, (size, size), 0)
    return [jnp.where(lower, jnp.concatenate(rows, axis=0), 0.0) for rows in stacks]


def call(kernel, out_shape, *args, smem=(), scratch=(), name=None, memory=pltpu.VMEM, grid_spec=None):
    specs = [pl.BlockSpec(memory_space=pltpu.SMEM if i in smem else memory) for i in range(len(args))]
    outs = jax.tree.map(lambda _: pl.BlockSpec(memory_space=memory), out_shape)
    return pl.pallas_call(
        kernel,
        out_shape=out_shape,
        in_specs=specs,
        out_specs=outs,
        scratch_shapes=scratch,
        compiler_params=pltpu.CompilerParams(vmem_limit_bytes=VMEM_BYTES),
        name=name,
    )(*args)


def f32(*shape):
    return jax.ShapeDtypeStruct(shape, jnp.float32)


def split_kernel(order, snapshots, *rest):
    outs, sems = rest[:-1], rest[-1]
    edges = outs[0].shape[-1]
    copies = []
    for k, out in enumerate(outs):
        chunk = order(k)
        columns = pl.ds(pl.multiple_of(chunk * edges, edges), edges)
        copies.append(pltpu.make_async_copy(snapshots.at[0, :, columns], out, sems.at[k]))
    for copy in copies:
        copy.start()
    for copy in copies:
        copy.wait()


def transposed_snapshots(snapshots, n):
    _, steps, edges = snapshots.shape
    edges = edges // n
    pairwise = n <= 8 and n & (n - 1) == 0
    if pairwise:
        order = lambda k: lax.axis_index("row") ^ k
    else:
        order = lambda k: k
    blocks = call(
        functools.partial(split_kernel, order),
        [f32(steps, edges)] * n,
        snapshots,
        scratch=[pltpu.SemaphoreType.DMA((n,))],
        memory=pl.ANY,
        name="split_edges",
    )
    if pairwise:
        got = [blocks[0]]
        for k in range(1, n):
            got.append(lax.ppermute(blocks[k], "row", [(i, i ^ k) for i in range(n)]))
        return got, order
    got = lax.all_to_all(jnp.stack(blocks), "row", 0, 0)
    return [got[k] for k in range(n)], order


def sketch_kernel(order, counts, sketch, *rest):
    blocks, active, product = rest[:-2], rest[-2], rest[-1]
    steps, edges = blocks[0].shape
    for k, block in enumerate(blocks):
        first = pl.multiple_of(order(k) * steps, steps)
        position = first + lax.broadcasted_iota(jnp.int32, (steps, edges), 0)
        valid = (position < counts[0]).astype(jnp.float32)
        active[pl.ds(first, steps), :] = block[...] * valid
    sketch_rows = dot(sketch[0], active[...], (0, 0))
    product[...] = dot(active[...], sketch_rows, (1, 1)).reshape(product.shape)


def powered_kernel(edge_count, sketch, product, active, powered):
    products = product[...].reshape(active.shape[0], -1)
    gram = dot(sketch[0], products, (0, 0))
    raw = dot(products, active[...], (0, 0))
    (inverse,) = inverse_cholesky([gram])
    powered[...] = dot(inverse, raw) / edge_count


def kernel_blocks_kernel(own, partner, out):
    rank = own.shape[0]
    half = rank // 2
    me = lax.axis_index("case")
    out[:rank, :] = dot(own[...], own[...], (1, 1))

    @pl.when(me == 0)
    def _():
        out[rank:, :] = dot(partner[:half, :], own[...], (1, 1))

    @pl.when(me == 1)
    def _():
        out[rank:, :] = dot(own[half:, :], partner[...], (1, 1))


def merge_kernel(scale_out, own_sums, partner_sums, own, partner, start, case_out, merged):
    rank = own.shape[0]
    first = lax.axis_index("case") == 0
    sums = jnp.where(first, own_sums[...], partner_sums[...]), jnp.where(first, partner_sums[...], own_sums[...])
    cross = jnp.concatenate([sums[0][rank:], sums[1][rank:]], axis=0)
    kernel = jnp.concatenate(
        [
            jnp.concatenate([sums[0][:rank], cross.T], axis=1),
            jnp.concatenate([cross, sums[1][:rank]], axis=1),
        ],
        axis=0,
    )
    vectors = start[...]
    for sweep_index in range(ITERS):
        vectors = dot(kernel, vectors)
        gram = dot(vectors, vectors, (0, 0))
        if sweep_index == 0:
            inverse, case_inverse = inverse_cholesky([gram, own_sums[:rank, :]])
            case_out[0] = dot(case_inverse, own[...]) * scale_out
        else:
            (inverse,) = inverse_cholesky([gram])
        vectors = dot(vectors, inverse, (1, 1))
    reduced = dot(vectors, dot(kernel, vectors), (0, 0))
    (inverse,) = inverse_cholesky([reduced])
    half = merged.shape[1]

    def project(columns):
        low = jnp.where(first, own[:, columns], partner[:, columns])
        high = jnp.where(first, partner[:, columns], own[:, columns])
        return dot(vectors, jnp.concatenate([low, high], axis=0), (0, 0))

    columns = pl.ds(pl.multiple_of(lax.axis_index("case") * half, half), half)
    merged[...] = dot(inverse, project(columns)) * scale_out


def sum_over_row(value, n):
    if n & (n - 1):
        return lax.psum(value, "row")
    apart = 1
    while apart < n:
        value = value + lax.ppermute(value, "row", [(i, i ^ apart) for i in range(n)])
        apart *= 2
    return value


def swapped(value):
    return lax.ppermute(value, "case", [(0, 1), (1, 0)])


def local(snapshots, counts, sketch, start_block):
    n = lax.axis_size("row")
    blocks, order = transposed_snapshots(snapshots, n)
    steps, edges = blocks[0].shape
    rank = sketch.shape[-1]
    edge_count = n * edges
    scale_out = math.sqrt(edge_count)
    active, product = call(
        functools.partial(sketch_kernel, order),
        [f32(n * steps, edges), f32(n, steps, rank)],
        counts,
        sketch,
        *blocks,
        smem=(0,),
        name="sketch_product",
    )
    part = jnp.sum(lax.all_to_all(product, "row", 0, 0), axis=0)
    product = lax.all_to_all(jnp.broadcast_to(part[None], (n, steps, rank)), "row", 0, 0)
    powered = call(
        functools.partial(powered_kernel, float(edge_count)), f32(rank, edges), sketch, product, active, name="powered"
    )
    partner = swapped(powered)
    sums = call(kernel_blocks_kernel, f32(rank + rank // 2, rank), powered, partner, name="kernel_blocks")
    sums = sum_over_row(sums, n)
    partner_sums = swapped(sums)
    case_out, merged = call(
        functools.partial(merge_kernel, scale_out),
        [f32(1, rank, edges), f32(rank, edges // 2)],
        sums,
        partner_sums,
        powered,
        partner,
        start_block,
        name="merge",
    )
    return case_out, merged


def solution(mesh):
    in_specs = (P(("grp", "case"), "row", None), P(("grp", "case")), P("case", None, None), P())
    out_specs = (P(("grp", "case"), None, "row"), P("grp", ("row", "case")))
    return jax.shard_map(local, mesh=mesh, in_specs=in_specs, out_specs=out_specs, check_vma=False)
```

time: 430 us -> 102 us (0.24)
  waiting for transfers between devices: 233 us -> 30.8 us
  other arithmetic: 138 us -> 0.05 us
  blocking collectives: 0 us -> 27.1 us
  Pallas kernels: 0 us -> 27 us
  matrix products: 16.3 us -> 0 us
  local copies, waits for them, and re-layouts: 14.9 us -> 1.29 us
  between operations: 15 us -> 1.4 us
  starting transfers between devices: 8.46 us -> 14.2 us
    psum x3 -> x0, waiting for transfers between devices: 207 us -> none  [the longest x1 70.6 us: local(): gram_two = lax.psum(jnp.dot(powered, powered.T, precision=precise), 'row')]
    another operation x25 -> x0, other arithmetic: 115 us -> none  [the longest x10 52.3 us: lower_solve(): return jax.scipy.linalg.solve_triangular(factor, matrix, lower=True)]
    ppermute x1 -> x12, waiting for transfers between devices: 0.5 us -> 30.8 us  [the longest x3 14.7 us: sum_over_row(): lax.ppermute(value, 'row', [(i, i ^ apart) for i in range(n)])]
    all_to_all x0 -> x2, blocking collectives: none -> 27.1 us  [the longest x1 15.9 us: local(): part = jnp.sum(lax.all_to_all(product, 'row', 0, 0), axis=0)]
    pallas_call x0 -> x5, Pallas kernels: none -> 27 us  [call(): pl.pallas_call(kernel, out_shape=out_shape, in_specs=specs, out_specs=out...]
    all_to_all x1 -> x0, waiting for transfers between devices: 24.7 us -> none  [local(): lax.all_to_all(snapshots, 'row', split_axis=2, concat_axis=1, tiled=True)[0]]
    unnamed x1 -> x0, other arithmetic: 19.4 us -> none
    ppermute x1 -> x12, starting transfers between devices: 0.07 us -> 14.2 us  [the longest x7 13.1 us: transposed_snapshots(): got.append(lax.ppermute(blocks[k], 'row', [(i, i ^ k) for i in range(n)]))]
  transfers between devices with their start and end apart: 5 -> 12, of which waited for: 5 -> 7; matrix products, arithmetic and copies ran while one was open for 0% -> 0% of each run, Pallas kernels for 0% -> 0%
where the time goes in v1:
time: 102 us
  waiting for transfers between devices  30.8 us (30%)
  blocking collectives  27.1 us (27%)
  Pallas kernels  27 us (26%)
  starting transfers between devices  14.2 us (14%)
  between operations  1.4 us (1%)
  local copies, waits for them, and re-layouts  1.29 us (1%)
    pallas_call x5, Pallas kernels, call(): pl.pallas_call(kernel, out_shape=out_shape, in_specs=specs, out_specs=out...  27 us
    all_to_all x1, blocking collectives, local(): part = jnp.sum(lax.all_to_all(product, 'row', 0, 0), axis=0)  15.9 us
    ppermute x3, waiting for transfers between devices, sum_over_row(): lax.ppermute(value, 'row', [(i, i ^ apart) for i in range(n)])  14.7 us
    ppermute x7, waiting for transfers between devices, transposed_snapshots(): got.append(lax.ppermute(blocks[k], 'row', [(i, i ^ k) for i in range(n)]))  13.2 us
    ppermute x7, starting transfers between devices, transposed_snapshots(): got.append(lax.ppermute(blocks[k], 'row', [(i, i ^ k) for i in range(n)]))  13.1 us
    all_to_all x1, blocking collectives, local(): lax.all_to_all(jnp.broadcast_to(part[None], (n, steps, rank)), 'row', 0, 0)  11.3 us
    ppermute x2, waiting for transfers between devices, swapped(): return lax.ppermute(value, 'case', [(0, 1), (1, 0)])  2.81 us
  transfers between devices with their start and end apart: 12, of which 7 were waited for; matrix products, arithmetic and copies ran while one was open for 0% of the time, Pallas kernels for 0%

profile of v1, /device:TPU:0, one launch (start us, length us, event | category | flops | bytes accessed | tf_op | source)
XLA Modules:
  0.0 101.8 jit_solution(17426103144392779643)
XLA Ops:
  0.6 1.3 %copy-done.1 = f32[1,64,4096]{2,1,0:T(8,128)S(1)} copy-done((f32[1,64,4096]{2,1,0:T(8,128)S(1)}, f32[1,64,4096]{2,1,0:T(8,128)}, u32[]{:S(2)}) %copy-start.1) | copy-done | bytes 1048600
  1.9 0.3 split_edges.1
  2.2 3.0 %collective-permute-start = (f32[64,512]{1,0:T(8,128)S(1)}, f32[64,512]{1,0:T(8,128)S(1)}, u32[]{:S(2)}, u32[]{:S(2)}) collective-permute-start(f32[64,512]{1,0:T(8,128)S(1)} %get-tuple-element.13), channel_id=1, source_target_pairs={{0,2},{2,0},{4,6},{6,4},{8,10},{10,8},{12,14},{14,12},{1,3},{3,1},... | collective-permute-start | bytes 393224 | tf_op jit(solution)/shard_map/ppermute | solution.py:114
  5.2 1.6 %collective-permute-start.1 = (f32[64,512]{1,0:T(8,128)S(1)}, f32[64,512]{1,0:T(8,128)S(1)}, u32[]{:S(2)}, u32[]{:S(2)}) collective-permute-start(f32[64,512]{1,0:T(8,128)S(1)} %get-tuple-element.14), channel_id=1, source_target_pairs={{0,4},{2,6},{4,0},{6,2},{8,12},{10,14},{12,8},{14,10},{1,5},{3,7},... | collective-permute-start | bytes 393224 | tf_op jit(solution)/shard_map/ppermute | solution.py:114
  6.8 3.0 %collective-permute-start.3 = (f32[64,512]{1,0:T(8,128)S(1)}, f32[64,512]{1,0:T(8,128)S(1)}, u32[]{:S(2)}, u32[]{:S(2)}) collective-permute-start(f32[64,512]{1,0:T(8,128)S(1)} %get-tuple-element.16), channel_id=1, source_target_pairs={{0,8},{2,10},{4,12},{6,14},{8,0},{10,2},{12,4},{14,6},{1,9},{3,11}... | collective-permute-start | bytes 393224 | tf_op jit(solution)/shard_map/ppermute | solution.py:114
  9.8 1.3 %collective-permute-start.4 = (f32[64,512]{1,0:T(8,128)S(1)}, f32[64,512]{1,0:T(8,128)S(1)}, u32[]{:S(2)}, u32[]{:S(2)}) collective-permute-start(f32[64,512]{1,0:T(8,128)S(1)} %get-tuple-element.17), channel_id=1, source_target_pairs={{0,10},{2,8},{4,14},{6,12},{8,2},{10,0},{12,6},{14,4},{1,11},{3,9}... | collective-permute-start | bytes 393224 | tf_op jit(solution)/shard_map/ppermute | solution.py:114
  11.1 3.6 %collective-permute-start.5 = (f32[64,512]{1,0:T(8,128)S(1)}, f32[64,512]{1,0:T(8,128)S(1)}, u32[]{:S(2)}, u32[]{:S(2)}) collective-permute-start(f32[64,512]{1,0:T(8,128)S(1)} %get-tuple-element.18), channel_id=1, source_target_pairs={{0,12},{2,14},{4,8},{6,10},{8,4},{10,6},{12,0},{14,2},{1,13},{3,15... | collective-permute-start | bytes 393224 | tf_op jit(solution)/shard_map/ppermute | solution.py:114
  14.7 1.3 %collective-permute-done.1.rest_2_ = f32[64,512]{1,0:T(8,128)S(1)} collective-permute-done((f32[64,512]{1,0:T(8,128)S(1)}, f32[64,512]{1,0:T(8,128)S(1)}, u32[]{:S(2)}, u32[]{:S(2)}) %collective-permute-start.1) | collective-permute-done | bytes 131104 | tf_op jit(solution)/shard_map/ppermute | solution.py:114
  15.9 0.7 collective-permute-start.6
  17.3 11.9 %collective-permute-done.4.rest_5_ = f32[64,512]{1,0:T(8,128)S(1)} collective-permute-done((f32[64,512]{1,0:T(8,128)S(1)}, f32[64,512]{1,0:T(8,128)S(1)}, u32[]{:S(2)}, u32[]{:S(2)}) %collective-permute-start.4) | collective-permute-done | bytes 131104 | tf_op jit(solution)/shard_map/ppermute | solution.py:114
  29.2 1.8 %sketch_product.1 = (f32[512,512]{1,0:T(8,128)S(1)}, f32[8,64,128]{2,1,0:T(8,128)S(1)}) custom-call(s32[1]{0:T(128)S(6)} %copy.6.counts, f32[1,512,128]{2,1,0:T(8,128)S(1)} %copy-done, f32[64,512]{1,0:T(8,128)S(1)} %get-tuple-element.12.rest_0_, f32[64,512]{1,0:T(8,128)S(1)} %collective-permute-done.rest_1_, f32[64,512]{1,0:T(8,128)S(1)} %collective-permute-done.1.rest_2_, ...), custom_call_target="tpu_custom_call" | custom-call | tf_op jit(solution)/shard_map/sketch_product/pallas_call | solution.py:66
  31.0 15.9 %all_to_all.10 = f32[8,64,128]{2,1,0:T(8,128)S(1)} all-to-all(f32[8,64,128]{2,1,0:T(8,128)S(1)} %get-tuple-element.20), channel_id=1, replica_groups=mesh['grp'=2,'row'=8,'case'=2] {'row'}, dimensions={0} | all-to-all | bytes 524288 | tf_op jit(solution)/shard_map/all_to_all | solution.py:220
  47.0 11.3 %all_to_all.11.product = f32[8,64,128]{2,1,0:T(8,128)S(1)} all-to-all(f32[8,64,128]{2,1,0:T(8,128)S(1)} %broadcast_in_dim.2), channel_id=1, replica_groups=mesh['grp'=2,'row'=8,'case'=2] {'row'}, dimensions={0} | all-to-all | bytes 524288 | tf_op jit(solution)/shard_map/all_to_all | solution.py:221
  58.2 5.6 %powered.1.own = f32[128,512]{1,0:T(8,128)S(1)} custom-call(f32[1,512,128]{2,1,0:T(8,128)S(1)} %copy-done, f32[8,64,128]{2,1,0:T(8,128)S(1)} %all_to_all.11.product, f32[512,512]{1,0:T(8,128)S(1)} %get-tuple-element.21.active), custom_call_target="tpu_custom_call" | custom-call | tf_op jit(solution)/shard_map/powered/pallas_call | solution.py:66
  63.9 1.5 %collective-permute-done.7.partner = f32[128,512]{1,0:T(8,128)S(1)} collective-permute-done((f32[128,512]{1,0:T(8,128)S(1)}, f32[128,512]{1,0:T(8,128)S(1)}, u32[]{:S(2)}, u32[]{:S(2)}) %collective-permute-start.7) | collective-permute-done | bytes 262176 | tf_op jit(solution)/shard_map/ppermute | solution.py:201
  65.4 0.9 kernel_blocks.1
  66.4 0.2 collective-permute-start.8
  66.6 4.7 %collective-permute-done.8 = f32[192,128]{1,0:T(8,128)S(1)} collective-permute-done((f32[192,128]{1,0:T(8,128)S(1)}, f32[192,128]{1,0:T(8,128)S(1)}, u32[]{:S(2)}, u32[]{:S(2)}) %collective-permute-start.8) | collective-permute-done | bytes 98336 | tf_op jit(solution)/shard_map/ppermute | solution.py:195
  71.3 0.1 collective-permute-start.9
  71.4 4.6 %collective-permute-done.9 = f32[192,128]{1,0:T(8,128)S(1)} collective-permute-done((f32[192,128]{1,0:T(8,128)S(1)}, f32[192,128]{1,0:T(8,128)S(1)}, u32[]{:S(2)}, u32[]{:S(2)}) %collective-permute-start.9) | collective-permute-done | bytes 98336 | tf_op jit(solution)/shard_map/ppermute | solution.py:195
  76.0 0.6 collective-permute-start.10
  76.7 5.4 %collective-permute-done.10 = f32[192,128]{1,0:T(8,128)S(1)} collective-permute-done((f32[192,128]{1,0:T(8,128)S(1)}, f32[192,128]{1,0:T(8,128)S(1)}, u32[]{:S(2)}, u32[]{:S(2)}) %collective-permute-start.10) | collective-permute-done | bytes 98336 | tf_op jit(solution)/shard_map/ppermute | solution.py:195
  82.2 1.3 %collective-permute-done.11.partner_sums = f32[192,128]{1,0:T(8,128)S(1)} collective-permute-done((f32[192,128]{1,0:T(8,128)S(1)}, f32[192,128]{1,0:T(8,128)S(1)}, u32[]{:S(2)}, u32[]{:S(2)}) %collective-permute-start.11) | collective-permute-done | bytes 98336 | tf_op jit(solution)/shard_map/ppermute | solution.py:201
  83.5 18.3 %merge.1 = (f32[1,128,512]{2,1,0:T(8,128)}, f32[128,256]{1,0:T(8,128)}) custom-call(f32[192,128]{1,0:T(8,128)S(1)} %add.11.own_sums, f32[192,128]{1,0:T(8,128)S(1)} %collective-permute-done.11.partner_sums, f32[128,512]{1,0:T(8,128)S(1)} %powered.1.own, f32[128,512]{1,0:T(8,128)S(1)} %collective-permute-done.7.partner, f32[256,128]{1,0:T(8,128)S(1)} %copy-done.2), custom_call_target="tpu_custom_call" | custom-call | tf_op jit(solution)/shard_map/merge/pallas_call | solution.py:66
  (18 shorter events, 0.2 us)
Async XLA Ops:
  0.6 28.6 %copy-start = (f32[1,512,128]{2,1,0:T(8,128)S(1)}, f32[1,512,128]{2,1,0:T(8,128)}, u32[]{:S(2)}) copy-start(f32[1,512,128]{2,1,0:T(8,128)} %sketch.3) | copy-start | bytes 786436
  0.6 1.3 %copy-start.1 = (f32[1,64,4096]{2,1,0:T(8,128)S(1)}, f32[1,64,4096]{2,1,0:T(8,128)}, u32[]{:S(2)}) copy-start(f32[1,64,4096]{2,1,0:T(8,128)} %snapshots.1) | copy-start | bytes 3145732
  2.2 8.9 %collective-permute-start = (f32[64,512]{1,0:T(8,128)S(1)}, f32[64,512]{1,0:T(8,128)S(1)}, u32[]{:S(2)}, u32[]{:S(2)}) collective-permute-start(f32[64,512]{1,0:T(8,128)S(1)} %get-tuple-element.13), channel_id=1, source_target_pairs={{0,2},{2,0},{4,6},{6,4},{8,10},{10,8},{12,14},{14,12},{1,3},{3,1},... | collective-permute-start | bytes 393224 | tf_op jit(solution)/shard_map/ppermute | solution.py:114
  5.2 10.7 %collective-permute-start.1 = (f32[64,512]{1,0:T(8,128)S(1)}, f32[64,512]{1,0:T(8,128)S(1)}, u32[]{:S(2)}, u32[]{:S(2)}) collective-permute-start(f32[64,512]{1,0:T(8,128)S(1)} %get-tuple-element.14), channel_id=1, source_target_pairs={{0,4},{2,6},{4,0},{6,2},{8,12},{10,14},{12,8},{14,10},{1,5},{3,7},... | collective-permute-start | bytes 393224 | tf_op jit(solution)/shard_map/ppermute | solution.py:114
  6.8 10.5 %collective-permute-start.2 = (f32[64,512]{1,0:T(8,128)S(1)}, f32[64,512]{1,0:T(8,128)S(1)}, u32[]{:S(2)}, u32[]{:S(2)}) collective-permute-start(f32[64,512]{1,0:T(8,128)S(1)} %get-tuple-element.15), channel_id=1, source_target_pairs={{0,6},{2,4},{4,2},{6,0},{8,14},{10,12},{12,10},{14,8},{1,7},{3,5},... | collective-permute-start | bytes 393224 | tf_op jit(solution)/shard_map/ppermute | solution.py:114
  6.8 10.5 %collective-permute-start.3 = (f32[64,512]{1,0:T(8,128)S(1)}, f32[64,512]{1,0:T(8,128)S(1)}, u32[]{:S(2)}, u32[]{:S(2)}) collective-permute-start(f32[64,512]{1,0:T(8,128)S(1)} %get-tuple-element.16), channel_id=1, source_target_pairs={{0,8},{2,10},{4,12},{6,14},{8,0},{10,2},{12,4},{14,6},{1,9},{3,11}... | collective-permute-start | bytes 393224 | tf_op jit(solution)/shard_map/ppermute | solution.py:114
  9.8 19.4 %collective-permute-start.4 = (f32[64,512]{1,0:T(8,128)S(1)}, f32[64,512]{1,0:T(8,128)S(1)}, u32[]{:S(2)}, u32[]{:S(2)}) collective-permute-start(f32[64,512]{1,0:T(8,128)S(1)} %get-tuple-element.17), channel_id=1, source_target_pairs={{0,10},{2,8},{4,14},{6,12},{8,2},{10,0},{12,6},{14,4},{1,11},{3,9}... | collective-permute-start | bytes 393224 | tf_op jit(solution)/shard_map/ppermute | solution.py:114
  11.1 18.2 %collective-permute-start.5 = (f32[64,512]{1,0:T(8,128)S(1)}, f32[64,512]{1,0:T(8,128)S(1)}, u32[]{:S(2)}, u32[]{:S(2)}) collective-permute-start(f32[64,512]{1,0:T(8,128)S(1)} %get-tuple-element.18), channel_id=1, source_target_pairs={{0,12},{2,14},{4,8},{6,10},{8,4},{10,6},{12,0},{14,2},{1,13},{3,15... | collective-permute-start | bytes 393224 | tf_op jit(solution)/shard_map/ppermute | solution.py:114
  15.9 13.3 %collective-permute-start.6 = (f32[64,512]{1,0:T(8,128)S(1)}, f32[64,512]{1,0:T(8,128)S(1)}, u32[]{:S(2)}, u32[]{:S(2)}) collective-permute-start(f32[64,512]{1,0:T(8,128)S(1)} %get-tuple-element.19), channel_id=1, source_target_pairs={{0,14},{2,12},{4,10},{6,8},{8,6},{10,4},{12,2},{14,0},{1,15},{3,13... | collective-permute-start | bytes 393224 | tf_op jit(solution)/shard_map/ppermute | solution.py:114
  63.8 1.6 %collective-permute-start.7 = (f32[128,512]{1,0:T(8,128)S(1)}, f32[128,512]{1,0:T(8,128)S(1)}, u32[]{:S(2)}, u32[]{:S(2)}) collective-permute-start(f32[128,512]{1,0:T(8,128)S(1)} %powered.1.own), channel_id=1, source_target_pairs={{0,1},{1,0},{2,3},{3,2},{4,5},{5,4},{6,7},{7,6},{8,9},{9,8},{10,11... | collective-permute-start | bytes 786440 | tf_op jit(solution)/shard_map/ppermute | solution.py:201
  66.4 4.9 %collective-permute-start.8 = (f32[192,128]{1,0:T(8,128)S(1)}, f32[192,128]{1,0:T(8,128)S(1)}, u32[]{:S(2)}, u32[]{:S(2)}) collective-permute-start(f32[192,128]{1,0:T(8,128)S(1)} %kernel_blocks.1), channel_id=1, source_target_pairs={{0,2},{2,0},{4,6},{6,4},{8,10},{10,8},{12,14},{14,12},{1,3},{3,1},... | collective-permute-start | bytes 294920 | tf_op jit(solution)/shard_map/ppermute | solution.py:195
  71.3 4.7 %collective-permute-start.9 = (f32[192,128]{1,0:T(8,128)S(1)}, f32[192,128]{1,0:T(8,128)S(1)}, u32[]{:S(2)}, u32[]{:S(2)}) collective-permute-start(f32[192,128]{1,0:T(8,128)S(1)} %add.9), channel_id=1, source_target_pairs={{0,4},{2,6},{4,0},{6,2},{8,12},{10,14},{12,8},{14,10},{1,5},{3,7},... | collective-permute-start | bytes 294920 | tf_op jit(solution)/shard_map/ppermute | solution.py:195
  76.0 7.5 %copy-start.2 = (f32[256,128]{1,0:T(8,128)S(1)}, f32[256,128]{1,0:T(8,128)}, u32[]{:S(2)}) copy-start(f32[256,128]{1,0:T(8,128)} %start.1) | copy-start | bytes 393220
  76.0 6.1 %collective-permute-start.10 = (f32[192,128]{1,0:T(8,128)S(1)}, f32[192,128]{1,0:T(8,128)S(1)}, u32[]{:S(2)}, u32[]{:S(2)}) collective-permute-start(f32[192,128]{1,0:T(8,128)S(1)} %add.10), channel_id=1, source_target_pairs={{0,8},{2,10},{4,12},{6,14},{8,0},{10,2},{12,4},{14,6},{1,9},{3,11}... | collective-permute-start | bytes 294920 | tf_op jit(solution)/shard_map/ppermute | solution.py:195
  82.1 1.4 %collective-permute-start.11 = (f32[192,128]{1,0:T(8,128)S(1)}, f32[192,128]{1,0:T(8,128)S(1)}, u32[]{:S(2)}, u32[]{:S(2)}) collective-permute-start(f32[192,128]{1,0:T(8,128)S(1)} %add.11.own_sums), channel_id=1, source_target_pairs={{0,1},{1,0},{2,3},{3,2},{4,5},{5,4},{6,7},{7,6},{8,9},{9,8},{10,11... | collective-permute-start | bytes 294920 | tf_op jit(solution)/shard_map/ppermute | solution.py:201
